TPU v7x, 32 devices: a whole 2x2x4 slice. The times are simulated.
32 devices in a mesh: seq: 4 (over x, core), blk: 8 (over z, y).
Axes of the slice: x: 2, y: 2, z: 4, core: 2. Of those that a mesh axis runs over, the one named last changes fastest.
Arguments:
- latents: bfloat16 [4, 8192, 512], P('seq', 'blk'), may hold values from -6 to 6
- tokens: bfloat16 [4, 8192, 512], P('seq', 'blk'), may hold values from -6 to 6
- lengths: int32 [4, 4], P('seq'), may hold values from 1792 to 2048, as said below
- gain_lat: float32 [512], replicated, may hold values from 0.1 to 1.9
- gain_tok: float32 [512], replicated, may hold values from 0.1 to 1.9
- gain_mlp: float32 [512], replicated, may hold values from 0.1 to 1.9
- w_query: bfloat16 [512, 512], replicated, may hold values from -0.625 to 0.625
- w_key: bfloat16 [512, 512], replicated, may hold values from -0.25 to 0.25
- w_value: bfloat16 [512, 512], replicated, may hold values from -0.25 to 0.25
- w_out: bfloat16 [512, 512], replicated, may hold values from -0.5 to 0.5
- w_up: bfloat16 [512, 2048], replicated, may hold values from -0.25 to 0.25
- w_down: bfloat16 [2048, 512], replicated, may hold values from -0.125 to 0.125
- d_out: bfloat16 [4, 8192, 512], P('seq', 'blk'), may hold values from -6 to 6
Outputs:
- out_latents: bfloat16 [4, 8192, 512], P('seq', 'blk')
- d_latents: float32 [4, 8192, 512], P('seq', 'blk')
- d_tokens: float32 [4, 8192, 512], P('seq', 'blk')
- d_w_query: float32 [512, 512], replicated
- d_w_key: float32 [512, 512], replicated
- d_w_value: float32 [512, 512], replicated
- d_w_out: float32 [512, 512], replicated
- d_w_up: float32 [512, 2048], replicated
- d_w_down: float32 [2048, 512], replicated
- d_gain_lat: float32 [512], replicated
- d_gain_tok: float32 [512], replicated
- d_gain_mlp: float32 [512], replicated
Inputs may be any that keep to these rules, and one draw needn't show every extreme that they name: Positions past the sum of a row's lengths are padding.
All inputs are finite; a program needn't handle non-finite values.
Results may differ from a plain program's by a relative error of at most 0.024.
Values may be sent and summed in bfloat16 or wider, within the bound.
No kernel may reach another device: no remote copies, remote signals or barrier semaphores. Data moves between devices by JAX's collectives and lax.ppermute only.
A program may use at most 256 MiB of HBM per device.

v0:
```python
import jax
import jax.numpy as jnp
from jax import lax
from jax.sharding import PartitionSpec as P

EPSILON = 1e-05
NEGATIVE = -1e30


def normed(values, gain):
    center = values - jnp.mean(values, axis=-1, keepdims=True)
    spread = jnp.mean(center * center, axis=-1, keepdims=True)
    return center * lax.rsqrt(spread + EPSILON) * gain


def dot_plain(left, right):
    return jnp.dot(left, right, preferred_element_type=jnp.float32)


def dot_rows(left, right):
    return lax.dot_general(
        left, right, (((1,), (1,)), ((), ())), preferred_element_type=jnp.float32
    )


def dot_first(left, right):
    return lax.dot_general(
        left, right, (((0,), (0,)), ((), ())), preferred_element_type=jnp.float32
    )


def scene_numbers(scene_lengths, first, count):
    bounds = jnp.cumsum(scene_lengths)
    places = first + jnp.arange(count, dtype=jnp.int32)
    return jnp.sum((places[:, None] >= bounds[None, :]).astype(jnp.int32), axis=1)


def scene_part(whole_rows, scene_count, scene_id):
    grid = whole_rows.reshape(
        (whole_rows.shape[0] // scene_count, scene_count) + whole_rows.shape[1:]
    )
    return lax.dynamic_index_in_dim(grid, scene_id, 1, keepdims=False)


def latent_order(stacked):
    moved = jnp.swapaxes(stacked, 0, 1)
    return moved.reshape((moved.shape[0] * moved.shape[1],) + moved.shape[2:])


def local(
    latents,
    tokens,
    lengths,
    gain_lat,
    gain_tok,
    gain_mlp,
    w_query,
    w_key,
    w_value,
    w_out,
    w_up,
    w_down,
    d_out,
):
    latent_rows = latents[0].astype(jnp.float32)
    token_rows = tokens[0].astype(jnp.float32)
    scene_lengths = lengths[0]
    scene_count = scene_lengths.shape[0]
    row_count = latent_rows.shape[0]
    span = token_rows.shape[0]
    width = latent_rows.shape[1]
    scale = width ** (-0.5)
    position = lax.axis_index("blk")
    lat_normed, lat_back = jax.vjp(normed, latent_rows, gain_lat)
    lat_low = lat_normed.astype(jnp.bfloat16)
    query = dot_plain(lat_low, w_query).astype(jnp.bfloat16)
    tok_normed, tok_back = jax.vjp(normed, token_rows, gain_tok)
    tok_low = tok_normed.astype(jnp.bfloat16)
    keys = dot_plain(tok_low, w_key).astype(jnp.bfloat16)
    values = dot_plain(tok_low, w_value).astype(jnp.bfloat16)
    own_segment = scene_numbers(scene_lengths, position * span, span)
    scene_ids = jnp.arange(scene_count, dtype=jnp.int32)
    all_query = lax.all_gather(query, "blk", axis=0, tiled=True)

    def forward_set(scene_id):
        query_set = scene_part(all_query, scene_count, scene_id)
        included = (own_segment == scene_id)[None, :]
        scores = jnp.where(included, dot_rows(query_set, keys) * scale, NEGATIVE)
        top = jnp.max(scores, axis=1)
        weights = jnp.where(included, jnp.exp(scores - top[:, None]), 0.0)
        return (top, jnp.sum(weights, axis=1), dot_plain(weights.astype(jnp.bfloat16), values))

    tops, totals, partial_sums = lax.map(forward_set, scene_ids)
    tops = latent_order(tops)
    totals = latent_order(totals)
    partial_sums = latent_order(partial_sums)
    peak = lax.pmax(tops.astype(jnp.bfloat16), "blk").astype(tops.dtype)
    factor = jnp.exp(tops - peak)
    own_sum, own_total = (
        lax.psum_scatter(
            (partial_sums * factor[:, None]).astype(jnp.bfloat16),
            "blk",
            scatter_dimension=0,
            tiled=True,
        ).astype(jnp.float32),
        lax.psum_scatter(
            (totals * factor).astype(jnp.bfloat16), "blk", scatter_dimension=0, tiled=True
        ).astype(jnp.float32),
    )
    own_peak = lax.dynamic_slice_in_dim(peak, position * row_count, row_count, 0)
    attended = own_sum / own_total[:, None]
    log_sum = own_peak + jnp.log(own_total)
    mixed = attended.astype(jnp.bfloat16)
    state = latent_rows + dot_plain(mixed, w_out)
    mlp_normed, mlp_back = jax.vjp(normed, state, gain_mlp)
    mlp_low = mlp_normed.astype(jnp.bfloat16)
    pre = dot_plain(mlp_low, w_up)
    activated, gelu_back = jax.vjp(jax.nn.gelu, pre)
    inner = activated.astype(jnp.bfloat16)
    output = (state + dot_plain(inner, w_down)).astype(jnp.bfloat16)
    cot_low = d_out[0]
    cotangent = cot_low.astype(jnp.float32)
    d_w_down = dot_first(inner, cot_low)
    d_inner = dot_rows(cot_low, w_down)
    d_pre = gelu_back(d_inner)[0].astype(jnp.bfloat16)
    d_w_up = dot_first(mlp_low, d_pre)
    d_mlp = dot_rows(d_pre, w_up)
    d_state_norm, d_gain_mlp = mlp_back(d_mlp)
    d_state = cotangent + d_state_norm
    d_proj = d_state.astype(jnp.bfloat16)
    d_w_out = dot_first(mixed, d_proj)
    d_attended = dot_rows(d_proj, w_out).astype(jnp.bfloat16)
    delta = jnp.sum(d_attended.astype(jnp.float32) * attended, axis=1)
    query_again, all_grad = (
        lax.all_gather(query, "blk", axis=0, tiled=True),
        lax.all_gather(d_attended, "blk", axis=0, tiled=True),
    )
    all_lse, all_delta = (
        lax.all_gather(log_sum, "blk", axis=0, tiled=True),
        lax.all_gather(delta, "blk", axis=0, tiled=True),
    )

    def backward_set(carried, scene_id):
        key_grad, value_grad = carried
        query_set = scene_part(query_again, scene_count, scene_id)
        grad_set = scene_part(all_grad, scene_count, scene_id)
        lse_set = scene_part(all_lse, scene_count, scene_id)
        delta_set = scene_part(all_delta, scene_count, scene_id)
        included = (own_segment == scene_id)[None, :]
        scores = jnp.where(included, dot_rows(query_set, keys) * scale, NEGATIVE)
        probs = jnp.where(included, jnp.exp(scores - lse_set[:, None]), 0.0)
        d_scores = (probs * (dot_rows(grad_set, values) - delta_set[:, None]) * scale).astype(
            jnp.bfloat16
        )
        key_grad = key_grad + dot_first(d_scores, query_set)
        value_grad = value_grad + dot_first(probs.astype(jnp.bfloat16), grad_set)
        return ((key_grad, value_grad), dot_plain(d_scores, keys))

    zeros_tok = jnp.zeros((span, width), jnp.float32)
    (d_keys, d_values), d_query_sets = lax.scan(backward_set, (zeros_tok, zeros_tok), scene_ids)
    d_query = lax.psum_scatter(
        latent_order(d_query_sets).astype(jnp.bfloat16), "blk", scatter_dimension=0, tiled=True
    )
    d_w_query = dot_first(lat_low, d_query)
    d_lat_part, d_gain_lat = lat_back(dot_rows(d_query, w_query))
    d_latents = d_state + d_lat_part
    d_key_low = d_keys.astype(jnp.bfloat16)
    d_value_low = d_values.astype(jnp.bfloat16)
    d_w_key = dot_first(tok_low, d_key_low)
    d_w_value = dot_first(tok_low, d_value_low)
    d_tok_norm = dot_rows(d_key_low, w_key) + dot_rows(d_value_low, w_value)
    d_tokens, d_gain_tok = tok_back(d_tok_norm)
    summed_grads = lax.psum(
        (
            d_w_query,
            d_w_key,
            d_w_value,
            d_w_out,
            d_w_up,
            d_w_down,
            d_gain_lat,
            d_gain_tok,
            d_gain_mlp,
        ),
        ("seq", "blk"),
    )
    return (
        output[None],
        d_latents[None],
        d_tokens[None],
        summed_grads[0],
        summed_grads[1],
        summed_grads[2],
        summed_grads[3],
        summed_grads[4],
        summed_grads[5],
        summed_grads[6],
        summed_grads[7],
        summed_grads[8],
    )


def solution(mesh):
    in_specs = (
        P("seq", "blk", None),
        P("seq", "blk", None),
        P("seq", None),
        P(),
        P(),
        P(),
        P(),
        P(),
        P(),
        P(),
        P(),
        P(),
        P("seq", "blk", None),
    )
    out_specs = (
        P("seq", "blk", None),
        P("seq", "blk", None),
        P("seq", "blk", None),
        P(),
        P(),
        P(),
        P(),
        P(),
        P(),
        P(),
        P(),
        P(),
    )
    return jax.shard_map(local, mesh=mesh, in_specs=in_specs, out_specs=out_specs, check_vma=False)
```

profile of v0, /device:TPU:0, one launch (start us, length us, event | category | flops | bytes accessed | tf_op | source)
XLA Modules:
  0.0 1296.0 jit_solution(1841367435203822853)
XLA Ops:
  19.3 120.9 %all-gather.3.cloned.1.call-done = bf16[8192,512]{1,0:T(8,128)(2,1)} async-done(((bf16[1024,512]{1,0:T(8,128)(2,1)}), bf16[8192,512]{1,0:T(8,128)(2,1)}) %all-gather.3.cloned.1.call-update) | async-done | bytes 8388624 | tf_op jit(solution)/shard_map/all_gather | solution.py:83
  140.3 12.6 reshape.185
  152.9 98.0 %while.33 = (s32[]{:T(128)}, f32[4,2048]{1,0:T(4,128)S(1)}, f32[4,2048]{1,0:T(4,128)S(1)}, f32[4,2048,512]{2,1,0:T(8,128)}, s32[4]{0:T(128)S(1)}, /*index=5*/s32...) while((s32[]{:T(128)}, f32[4,2048]{1,0:T(4,128)S(1)}, ...), condition=%wide.wide.region_9.10_spmd.clone, body=%wide.wide.region_6.9_spmd.sunk.clone | while | flops 4322227200 | bytes 75571424 | solution.py:93
  156.1 6.2 constant_dynamic-slice_fusion.9
  164.9 2.9 fusion.180
  168.3 9.0 bitcast_dynamic-update-slice_fusion.8
  180.5 6.2 constant_dynamic-slice_fusion.9
  189.3 2.9 fusion.180
  192.8 9.1 bitcast_dynamic-update-slice_fusion.8
  205.1 6.2 constant_dynamic-slice_fusion.9
  213.9 2.9 fusion.180
  217.3 9.1 bitcast_dynamic-update-slice_fusion.8
  229.6 6.2 constant_dynamic-slice_fusion.9
  238.4 2.9 fusion.180
  241.8 9.0 bitcast_dynamic-update-slice_fusion.8
  250.9 21.1 %copy.75 = f32[2048,4,512]{2,1,0:T(4,128)} copy(f32[2048,4,512]{2,0,1:T(8,128)} %bitcast.219) | data formatting | bytes 33554432 | tf_op jit(solution)/shard_map/transpose | solution.py:46
  272.0 19.4 %reshape.175 = f32[8192,512]{1,0:T(8,128)} reshape(f32[2048,4,512]{2,1,0:T(4,128)} %copy.75) | data formatting | bytes 33554432 | tf_op jit(solution)/shard_map/reshape | solution.py:47
  291.4 17.5 %copy.77 = f32[8192,512]{0,1:T(8,128)} copy(f32[8192,512]{1,0:T(8,128)} %reshape.175) | data formatting | bytes 33554432 | tf_op jit(solution)/shard_map/reshape | solution.py:47
  309.9 34.2 %pmax.7 = bf16[8192]{0:T(1024)(128)(2,1)S(1)} all-reduce(bf16[8192]{0:T(1024)(128)(2,1)S(1)} %convert_element_type.109), channel_id=1, replica_groups=mesh['seq'=4,'blk'=8] {'blk'}, use_global_device_ids=true, to_apply=%region_10.11 | all-reduce | flops 8192 | bytes 32768 | tf_op jit(solution)/shard_map/pmax | solution.py:97
  345.1 9.5 multiply_convert_fusion.1
  358.3 35.0 %all-reduce = bf16[8192]{0:T(1024)(128)(2,1)S(1)} all-reduce(bf16[8192]{0:T(1024)(128)(2,1)S(1)} %get-tuple-element.349), channel_id=3, replica_groups=mesh['seq'=4,'blk'=8] {'blk'}, use_global_device_ids=true, to_apply=%region_12.13.clone | all-reduce | flops 8192 | bytes 32768
  393.3 109.0 %reduce-scatter.3.cloned.1.call-done = bf16[1024,512]{0,1:T(8,128)(2,1)} async-done(((bf16[8192,512]{0,1:T(8,128)(2,1)}), bf16[1024,512]{0,1:T(8,128)(2,1)}) %reduce-scatter.3.cloned.1.call-update) | async-done | bytes 1048592 | tf_op jit(solution)/shard_map/reduce_scatter | solution.py:100
  507.7 7.4 fusion.47
  515.1 3.3 multiply_reduce_fusion
  523.0 3.9 broadcast_convert_fusion
  526.9 12.7 reshape.188
  539.7 30.9 %all_gather.14 = f32[8192]{0:T(1024)S(1)} all-gather(f32[1024]{0:T(1024)S(1)} %log_add_fusion), channel_id=1, replica_groups=mesh['seq'=4,'blk'=8] {'blk'}, dimensions={0}, use_global_device_ids=true | all-gather | bytes 36864 | tf_op jit(solution)/shard_map/all_gather | solution.py:139
  570.5 31.0 %all_gather.16 = f32[8192]{0:T(1024)S(1)} all-gather(f32[1024]{0:T(1024)S(1)} %get-tuple-element.360), channel_id=1, replica_groups=mesh['seq'=4,'blk'=8] {'blk'}, dimensions={0}, use_global_device_ids=true | all-gather | bytes 36864 | tf_op jit(solution)/shard_map/all_gather | solution.py:140
  601.5 46.3 %all-gather.5.cloned.1.call-done = bf16[8192,512]{0,1:T(8,128)(2,1)} async-done(((bf16[1024,512]{0,1:T(8,128)(2,1)}), bf16[8192,512]{0,1:T(8,128)(2,1)}) %all-gather.5.cloned.1.call-update) | async-done | bytes 8388624 | tf_op jit(solution)/shard_map/all_gather | solution.py:136
  647.8 12.0 copy.81
  659.8 12.6 reshape.187
  672.4 188.3 %while.34 = (s32[]{:T(128)}, f32[1024,512]{1,0:T(8,128)}, f32[1024,512]{1,0:T(8,128)}, bf16[4,2048,512]{2,1,0:T(8,128)(2,1)}, s32[4]{0:T(128)S(1)}, /*index=5*/s...) while((s32[]{:T(128)}, f32[1024,512]{1,0:T(8,128)}, ...), condition=%wide.wide.region_19.20_spmd.clone.clone, body=%wide.wide.region_18.19_spmd.clone.sunk.clone | while | flops 10766779392 | bytes 171113936 | solution.py:160
  689.2 10.4 constant_dynamic-slice_fusion.10
  699.7 5.6 fusion.191
  705.4 6.5 select_add_fusion.9
  711.9 7.0 multiply_convert_fusion.12
  723.9 3.2 copy-done.5
  733.7 10.4 constant_dynamic-slice_fusion.10
  744.2 5.6 fusion.191
  749.8 6.5 select_add_fusion.9
  756.4 7.0 multiply_convert_fusion.12
  768.4 3.2 copy-done.5
  778.2 10.4 constant_dynamic-slice_fusion.10
  788.6 5.6 fusion.191
  794.3 6.5 select_add_fusion.9
  800.9 7.0 multiply_convert_fusion.12
  812.9 3.2 copy-done.5
  822.6 10.4 constant_dynamic-slice_fusion.10
  833.1 5.6 fusion.191
  838.8 6.5 select_add_fusion.9
  845.4 7.0 multiply_convert_fusion.12
  857.4 3.2 copy-done.5
  860.8 12.3 copy.82
  873.0 12.6 convert_element_type.126
  886.8 3.1 fusion.92
  890.0 7.5 fusion.95
  897.5 4.7 fusion.74
  905.8 127.2 %reduce-scatter.5.cloned.1.call-done = bf16[1024,512]{1,0:T(8,128)(2,1)} async-done(((bf16[8192,512]{1,0:T(8,128)(2,1)}), bf16[1024,512]{1,0:T(8,128)(2,1)}) %reduce-scatter.5.cloned.1.call-update) | async-done | bytes 1048592 | tf_op jit(solution)/shard_map/reduce_scatter | solution.py:161
  1033.0 3.0 fusion.86
  1035.9 8.0 fusion.72
  1057.6 3.5 add_bitcast_fusion
  1061.2 2.9 copy.85
  1064.1 40.9 %all-reduce.1 = (f32[512]{0:T(512)}, f32[512]{0:T(512)}, f32[512]{0:T(512)}) all-reduce(f32[512]{0:T(512)S(1)} %get-tuple-element.294, f32[512]{0:T(512)S(1)} %get-tuple-element.367, f32[512]{0:T(512)S(1)} %copy-done.61), channel_id=1, replica_groups=mesh['seq'=4,'blk'=8] {'seq','blk'}, use_global_device_ids=true, to_apply=%region_32.33 | all-reduce | flops 1536 | bytes 12288 | tf_op jit(solution)/shard_map/psum | solution.py:173
  1105.0 171.7 %all-reduce.5.cloned.1.call-done = (f32[512,512]{1,0:T(8,128)}, f32[512,512]{1,0:T(8,128)}, f32[512,512]{1,0:T(8,128)}, f32[512,512]{1,0:T(8,128)}, f32[512,2048]{1,0:T(8,128)}, /*index=5*/f32[2048,512]{1,0:T(8,128)}) async-done(((f32[512,512]{1,0:T(8,128)}, f32[512,512]{1,0:T(8,128)}, f32[512,512]{1,0:T(8,128)}, f32[512,512]{1,0:T(8,128)}, f32[512,2048]{1,0:T(8,128)}, /*index=5*/f32[2048,512]{1,0:T(8,128)}), ...) | async-done | bytes 12582928 | tf_op jit(solution)/shard_map/psum | solution.py:173
  (346 shorter events, 112.7 us)
Async XLA Ops:
  7.2 497.6 %copy-start = (bf16[512,2048]{1,0:T(8,128)(2,1)S(1)}, bf16[512,2048]{1,0:T(8,128)(2,1)}, u32[]{:S(2)}) copy-start(bf16[512,2048]{1,0:T(8,128)(2,1)} %param.27) | copy-start | bytes 6291460
  7.2 3.4 copy-start.55
  7.2 133.1 %all-gather.3.cloned.1.call-start = ((), (), s32[]{:S(2)}) async-start(), calls=%async_computation.2 | async-start | bytes 9437184 | tf_op jit(solution)/shard_map/all_gather | solution.py:83
  8.9 3.6 copy-start.6
  12.5 489.8 %reduce-scatter.3.cloned.1.call-start = ((), (), s32[]{:S(2)}) async-start(), calls=%async_computation.3 | async-start | bytes 9437184 | tf_op jit(solution)/shard_map/reduce_scatter | solution.py:100
  156.1 6.2 copy-start.70
  180.5 6.2 copy-start.70
  205.1 6.2 copy-start.70
  229.6 6.2 copy-start.70
  354.6 147.7 %copy-start.7 = (bf16[1,1024,512]{1,2,0:T(8,128)(2,1)S(1)}, bf16[1,1024,512]{1,2,0:T(8,128)(2,1)}, u32[]{:S(2)}) copy-start(bf16[1,1024,512]{1,2,0:T(8,128)(2,1)} %copy-done.6) | copy-start | bytes 3145732
  354.6 293.2 %all-gather.5.cloned.1.call-start = ((), (), s32[]{:S(2)}) async-start(), calls=%async_computation.4 | async-start | bytes 9437184 | tf_op jit(solution)/shard_map/all_gather | solution.py:136
  393.3 126.8 %copy-start.57 = (f32[1024]{0:T(1024)}, f32[1024]{0:T(1024)S(1)}, u32[]{:S(2)}) copy-start(f32[1024]{0:T(1024)S(1)} %dynamic-slice_convert_fusion) | copy-start | bytes 12292
  504.4 14.1 %copy-start.14 = (f32[1024,512]{0,1:T(8,128)}, f32[1024,512]{0,1:T(8,128)S(1)}, u32[]{:S(2)}) copy-start(f32[1024,512]{0,1:T(8,128)S(1)} %get-tuple-element.358) | copy-start | bytes 6291460
  504.4 14.0 %copy-start.49 = (f32[1024]{0:T(1024)}, f32[1024]{0:T(1024)S(1)}, u32[]{:S(2)}) copy-start(f32[1024]{0:T(1024)S(1)} %broadcast_multiply_fusion) | copy-start | bytes 12292
  505.1 13.4 %copy-start.53 = (f32[1024]{0:T(1024)}, f32[1024]{0:T(1024)S(1)}, u32[]{:S(2)}) copy-start(f32[1024]{0:T(1024)S(1)} %fusion.91) | copy-start | bytes 12292
  507.7 7.4 copy-start.73
  523.0 510.0 %reduce-scatter.5.cloned.1.call-start = ((), (), s32[]{:S(2)}) async-start(), calls=%async_computation.5 | async-start | bytes 9437184 | tf_op jit(solution)/shard_map/reduce_scatter | solution.py:161
  689.2 10.5 copy-start.71
  699.7 5.7 copy-start.18
  705.3 6.6 copy-start.69
  705.3 16.1 %slice-start = ((s8[8388608]{0:T(1024)(128)(4,1)}), s8[4194304]{0:T(1024)(128)(4,1)S(1)}, s32[]{:S(2)}) async-start(s8[8388608]{0:T(1024)(128)(4,1)} %bitcast.216), calls=%async_computation.7 | async-start | bytes 8388608 | tf_op jit(solution)/shard_map/while
  711.9 7.0 copy-start.19
  711.9 7.0 copy-start.22
  711.9 9.6 slice-start.1
  733.7 10.5 copy-start.71
  744.2 5.7 copy-start.18
  749.8 6.5 copy-start.69
  749.8 16.1 %slice-start = ((s8[8388608]{0:T(1024)(128)(4,1)}), s8[4194304]{0:T(1024)(128)(4,1)S(1)}, s32[]{:S(2)}) async-start(s8[8388608]{0:T(1024)(128)(4,1)} %bitcast.216), calls=%async_computation.7 | async-start | bytes 8388608 | tf_op jit(solution)/shard_map/while
  756.4 7.0 copy-start.19
  756.4 7.0 copy-start.22
  756.4 9.6 slice-start.1
  778.2 10.5 copy-start.71
  788.6 5.7 copy-start.18
  794.3 6.5 copy-start.69
  794.3 16.1 %slice-start = ((s8[8388608]{0:T(1024)(128)(4,1)}), s8[4194304]{0:T(1024)(128)(4,1)S(1)}, s32[]{:S(2)}) async-start(s8[8388608]{0:T(1024)(128)(4,1)} %bitcast.216), calls=%async_computation.7 | async-start | bytes 8388608 | tf_op jit(solution)/shard_map/while
  800.8 7.0 copy-start.19
  800.9 7.0 copy-start.22
  800.9 9.6 slice-start.1
  822.6 10.5 copy-start.71
  833.1 5.7 copy-start.18
  838.8 6.5 copy-start.69
  838.8 16.1 %slice-start = ((s8[8388608]{0:T(1024)(128)(4,1)}), s8[4194304]{0:T(1024)(128)(4,1)S(1)}, s32[]{:S(2)}) async-start(s8[8388608]{0:T(1024)(128)(4,1)} %bitcast.216), calls=%async_computation.7 | async-start | bytes 8388608 | tf_op jit(solution)/shard_map/while
  845.3 7.0 copy-start.19
  845.3 7.0 copy-start.22
  845.3 9.6 slice-start.1
  885.6 4.3 copy-start.15
  885.6 4.3 copy-start.50
  885.6 4.3 copy-start.54
  885.6 4.3 copy-start.60
  885.7 391.1 %all-reduce.5.cloned.1.call-start = ((), (), s32[]{:S(2)}) async-start(), calls=%async_computation.6 | async-start | bytes 25165824 | tf_op jit(solution)/shard_map/psum | solution.py:173
  886.8 10.7 slice-start.2
  889.9 7.5 copy-start.28
  890.0 7.5 slice-start.3
  897.5 4.7 copy-start.4
  897.5 4.7 copy-start.24
  897.5 4.7 copy-start.36
  897.5 4.7 copy-start.42
  897.5 4.7 copy-start.52
  904.0 129.0 %copy-start.8 = (bf16[1,1024,512]{1,2,0:T(8,128)(2,1)S(1)}, bf16[1,1024,512]{1,2,0:T(8,128)(2,1)}, u32[]{:S(2)}) copy-start(bf16[1,1024,512]{1,2,0:T(8,128)(2,1)} %copy-done.6) | copy-start | bytes 3145732
  904.0 129.0 %copy-start.38 = (f32[1024]{0:T(1024)S(1)}, f32[1024]{0:T(1024)}, u32[]{:S(2)}) copy-start(f32[1024]{0:T(1024)} %copy-done.37) | copy-start | bytes 12292
  904.0 129.0 %copy-start.40 = (f32[1024]{0:T(1024)S(1)}, f32[1024]{0:T(1024)}, u32[]{:S(2)}) copy-start(f32[1024]{0:T(1024)} %copy-done.39) | copy-start | bytes 12292
  904.0 129.0 %copy-start.56 = (f32[512]{0:T(512)S(1)}, f32[512]{0:T(512)}, u32[]{:S(2)}) copy-start(f32[512]{0:T(512)} %param.20) | copy-start | bytes 6148
  1276.7 4.4 copy-start.29
  1282.3 3.7 copy-start.16
  (53 other events, 112.4 us)
Sparse Core Ops, SparseCore 0:
  12.6 127.6 all-gather.2
  354.7 147.4 reduce-scatter.2
  523.1 124.7 all-gather.4
  885.7 147.1 reduce-scatter.4
  1040.4 236.3 all-reduce.4
where the time goes:
time: 1310 us; the launch traced here: 1300 us
  waiting for transfers between devices  575 us (44%)
  local copies, waits for them, and re-layouts  266 us (20%)
  matrix products  200 us (15%)
  blocking collectives  172 us (13%)
  other arithmetic  40.9 us (3%)
  loops' own time  27 us (2%)
  between operations  15.6 us (1%)
    psum x1, waiting for transfers between devices, local(): lax.psum((d_w_query, d_w_key, d_w_value, d_w_out, d_w_up, d_w_down, d_gai...  172 us
    reduce_scatter x1, waiting for transfers between devices, local(): lax.psum_scatter(latent_order(d_query_sets).astype(jnp.bfloat16), 'blk',...  127 us
    all_gather x1, waiting for transfers between devices, local(): all_query = lax.all_gather(query, 'blk', axis=0, tiled=True)  121 us
    reduce_scatter x1, waiting for transfers between devices, local(): lax.psum_scatter((partial_sums * factor[:, None]).astype(jnp.bfloat16), '...  109 us
    dot_general x18, matrix products, dot_rows(): lax.dot_general(left, right, (((1,), (1,)), ((), ())), preferred_element_...  77.6 us
    dynamic_slice x12, local copies, waits for them, and re-layouts, scene_part(): return lax.dynamic_index_in_dim(grid, scene_id, 1, keepdims=False)  71.2 us
    dot_general x14, matrix products, dot_plain(): return jnp.dot(left, right, preferred_element_type=jnp.float32)  64 us
    dot_general x14, matrix products, dot_first(): lax.dot_general(left, right, (((0,), (0,)), ((), ())), preferred_element_...  58 us
  transfers between devices with their start and end apart: 5, of which 5 were waited for; matrix products, arithmetic and copies ran while one was open for 6% of the time, Pallas kernels for 0%

commit v1 on v0

v1 whole, which is shorter than its diff:
```python
import functools
import math

import jax
import jax.numpy as jnp
from jax import lax
from jax.experimental import pallas as pl
from jax.experimental.pallas import tpu as pltpu
from jax.sharding import PartitionSpec as P

EPSILON = 1e-05
NEGATIVE = -1e30
LOG2E = 1.4426950408889634
GELU_C = math.sqrt(2.0 / math.pi)
GELU_A = 0.044715
F32 = jnp.float32
BF16 = jnp.bfloat16
NN = (((1,), (0,)), ((), ()))
NT = (((1,), (1,)), ((), ()))
TN = (((0,), (0,)), ((), ()))
TILE = 256
VMEM_LIMIT = 60 << 20


def dot(left, right, dims=NN):
    return lax.dot_general(left, right, dims, preferred_element_type=F32)


def params():
    return pltpu.CompilerParams(vmem_limit_bytes=VMEM_LIMIT)


def whole(shape):
    zeros = (0,) * len(shape)
    return pl.BlockSpec(shape, lambda *_: zeros, pipeline_mode=pl.Buffered(1))


def norm_parts(rows):
    center = rows - jnp.mean(rows, axis=-1, keepdims=True)
    spread = jnp.mean(center * center, axis=-1, keepdims=True)
    inverse = lax.rsqrt(spread + EPSILON)
    return center * inverse, inverse


def norm_back(d_normed, unit, inverse, gain):
    d_unit = d_normed * gain
    mean_d = jnp.mean(d_unit, axis=-1, keepdims=True)
    mean_p = jnp.mean(d_unit * unit, axis=-1, keepdims=True)
    return inverse * (d_unit - mean_d - unit * mean_p)


def kv_kernel(tok_ref, gain_ref, wk_ref, wv_ref, k_ref, v_ref):
    unit, _ = norm_parts(tok_ref[...].astype(F32))
    low = (unit * gain_ref[...]).astype(BF16)
    k_ref[...] = dot(low, wk_ref[...]).astype(BF16)
    v_ref[...] = dot(low, wv_ref[...]).astype(BF16)


def keys_values(tok, gain, w_key, w_value):
    rows, width = tok.shape
    block = pl.BlockSpec((TILE, width), lambda i: (i, 0))
    shape = jax.ShapeDtypeStruct((rows, width), BF16)
    return pl.pallas_call(
        kv_kernel,
        grid=(rows // TILE,),
        in_specs=[block, whole(gain.shape), whole(w_key.shape), whole(w_value.shape)],
        out_specs=[block, block],
        out_shape=[shape, shape],
        compiler_params=params(),
        name="keys_values",
    )(tok, gain, w_key, w_value)


def forward_kernel(pieces, scale, info_ref, lat_ref, gl_ref, gm_ref, wq_ref, wo_ref, wu_ref, wd_ref, *refs):
    count = len(pieces)
    k_refs, v_refs = refs[:count], refs[count : 2 * count]
    refs = refs[2 * count :]
    q_ref, mixed_ref, mlp_ref, state_ref, inner_ref, slope_ref, out_ref, inv_ref = refs[:8]
    w_refs, refs = refs[8 : 8 + count], refs[8 + count :]
    s_refs, acc_ref = refs[:count], refs[count]
    rows = lat_ref.shape[0]
    begin, end = info_ref[0], info_ref[1]
    lat = lat_ref[...].astype(F32)
    unit, _ = norm_parts(lat)
    query = dot((unit * gl_ref[...]).astype(BF16), wq_ref[...]).astype(BF16)
    q_ref[...] = query
    top = jnp.full((8, rows), NEGATIVE, F32)
    for p in range(count):

        def scores(t, top, p=p):
            span = pl.ds(pl.multiple_of(t * TILE, TILE), TILE)
            s = dot(k_refs[p][span, :], query, NT) * (scale * LOG2E)
            place = info_ref[2 + 3 * p] + t * TILE + lax.broadcasted_iota(jnp.int32, (TILE, 1), 0)
            s = s + jnp.where((place >= begin) & (place < end), 0.0, NEGATIVE)
            s_refs[p][span, :] = s
            return jnp.maximum(top, jnp.max(s.reshape(TILE // 8, 8, rows), axis=0))

        top = lax.fori_loop(info_ref[3 + 3 * p], info_ref[4 + 3 * p], scores, top)
    top = jnp.max(top, axis=0, keepdims=True)
    total = jnp.zeros((8, rows), F32)
    acc_ref[...] = jnp.zeros_like(acc_ref)
    for p in range(count):

        def weigh(t, total, p=p):
            span = pl.ds(pl.multiple_of(t * TILE, TILE), TILE)
            w = jnp.exp2(s_refs[p][span, :] - top)
            low = w.astype(BF16)
            w_refs[p][span, :] = low
            acc_ref[...] += dot(low, v_refs[p][span, :], TN)
            return total + jnp.sum(w.reshape(TILE // 8, 8, rows), axis=0)

        total = lax.fori_loop(info_ref[3 + 3 * p], info_ref[4 + 3 * p], weigh, total)
    inverse = 1.0 / jnp.sum(total, axis=0, keepdims=True)
    inv_col = jnp.transpose(jnp.broadcast_to(inverse, (8, rows)))[:, :1]
    inv_ref[...] = jnp.broadcast_to(inv_col, inv_ref.shape)
    mixed = (acc_ref[...] * inv_col).astype(BF16)
    mixed_ref[...] = mixed
    state = lat + dot(mixed, wo_ref[...])
    state_ref[...] = state
    unit, _ = norm_parts(state)
    low = (unit * gm_ref[...]).astype(BF16)
    mlp_ref[...] = low
    out = state
    hidden = wu_ref.shape[1]
    step = min(512, hidden)
    for f in range(0, hidden, step):
        u = dot(low, wu_ref[:, f : f + step])
        square = u * u
        t = jnp.tanh(GELU_C * (u + GELU_A * (square * u)))
        half = 0.5 * (1.0 + t)
        inner = (u * half).astype(BF16)
        slope = half + (0.5 * GELU_C) * u * (1.0 - t * t) * (1.0 + 3.0 * GELU_A * square)
        inner_ref[:, f : f + step] = inner
        slope_ref[:, f : f + step] = slope.astype(BF16)
        out = out + dot(inner, wd_ref[f : f + step, :])
    out_ref[...] = out.astype(BF16)


def forward(info, lat, gl, gm, wq, wo, wu, wd, keys, values, scale):
    rows, width = lat.shape
    hidden = wu.shape[1]
    chunk = min(rows, TILE)
    pieces = [k.shape[0] for k in keys]

    def by_rows(columns):
        return pl.BlockSpec((chunk, columns), lambda i, *_: (i, 0))

    def shape(columns, dtype=BF16):
        return jax.ShapeDtypeStruct((rows, columns), dtype)

    return pl.pallas_call(
        functools.partial(forward_kernel, pieces, scale),
        grid_spec=pltpu.PrefetchScalarGridSpec(
            num_scalar_prefetch=1,
            grid=(rows // chunk,),
            in_specs=[by_rows(width)]
            + [whole(a.shape) for a in (gl, gm, wq, wo, wu, wd)]
            + [whole(a.shape) for a in (*keys, *values)],
            out_specs=[
                by_rows(width),
                by_rows(width),
                by_rows(width),
                by_rows(width),
                by_rows(hidden),
                by_rows(hidden),
                by_rows(width),
                by_rows(128),
            ]
            + [pl.BlockSpec((n, chunk), lambda i, *_: (0, i)) for n in pieces],
            scratch_shapes=[pltpu.VMEM((n, chunk), F32) for n in pieces] + [pltpu.VMEM((chunk, width), F32)],
        ),
        out_shape=[
            shape(width),
            shape(width),
            shape(width),
            shape(width, F32),
            shape(hidden),
            shape(hidden),
            shape(width),
            shape(128, F32),
        ]
        + [jax.ShapeDtypeStruct((n, rows), BF16) for n in pieces],
        compiler_params=params(),
        name="forward",
    )(info, lat, gl, gm, wq, wo, wu, wd, *keys, *values)


def mlp_back_kernel(
    chunks,
    slabs,
    cot_ref,
    slope_ref,
    state_ref,
    mixed_ref,
    mlp_ref,
    inner_ref,
    inv_ref,
    gm_ref,
    wo_ref,
    wu_ref,
    wd_ref,
    dstate_ref,
    datt_ref,
    delta_ref,
    pack_ref,
    dwo_ref,
    dgain_ref,
    dpre_ref,
    dproj_ref,
):
    i = pl.program_id(0)
    chunk = slope_ref.shape[0]
    hidden = wu_ref.shape[1]
    step = hidden // slabs

    @pl.when(i < chunks)
    def _():
        span = pl.ds(pl.multiple_of(i * chunk, chunk), chunk)
        cot = cot_ref[span, :]
        d_mlp = jnp.zeros(state_ref.shape, F32)
        for f in range(0, hidden, step):
            d_inner = dot(cot, wd_ref[f : f + step, :], NT)
            d_pre = (slope_ref[:, f : f + step].astype(F32) * d_inner).astype(BF16)
            dpre_ref[span, f : f + step] = d_pre
            d_mlp = d_mlp + dot(d_pre, wu_ref[:, f : f + step], NT)
        unit, inverse = norm_parts(state_ref[...])
        part = jnp.sum((d_mlp * unit).reshape(chunk // 8, 8, d_mlp.shape[1]), axis=0)
        dgain_ref[...] = jnp.where(i == 0, part, dgain_ref[...] + part)
        d_state = cot.astype(F32) + norm_back(d_mlp, unit, inverse, gm_ref[...])
        dstate_ref[...] = d_state
        d_proj = d_state.astype(BF16)
        dproj_ref[span, :] = d_proj
        d_att = (dot(d_proj, wo_ref[...], NT) * inv_ref[:, :1]).astype(BF16)
        datt_ref[...] = d_att
        delta = jnp.sum(d_att.astype(F32) * mixed_ref[span, :].astype(F32), axis=-1, keepdims=True)
        delta_ref[...] = jnp.transpose(jnp.broadcast_to(delta, (chunk, 128)))[:8, :]

    for j in range(slabs):

        @pl.when(i == chunks + j)
        def _(j=j):
            pack_ref[...] = dot(inner_ref[:, j * step : (j + 1) * step], cot_ref[...], TN).astype(BF16)

        @pl.when(i == chunks + slabs + j)
        def _(j=j):
            pack_ref[...] = dot(mlp_ref[...], dpre_ref[:, j * step : (j + 1) * step], TN).astype(BF16)

    @pl.when(i == chunks + 2 * slabs)
    def _():
        dwo_ref[...] = dot(mixed_ref[...], dproj_ref[...], TN).astype(BF16)


def mlp_back(cot, slope, state, mixed, mlp, inner, inv, gm, wo, wu, wd):
    rows, width = cot.shape
    hidden = wu.shape[1]
    slabs = hidden // width
    chunk = min(rows, TILE)
    chunks = rows // chunk

    def by_rows(columns):
        return pl.BlockSpec((chunk, columns), lambda i: (jnp.minimum(i, chunks - 1), 0))

    return pl.pallas_call(
        functools.partial(mlp_back_kernel, chunks, slabs),
        grid=(chunks + 2 * slabs + 1,),
        in_specs=[
            whole(cot.shape),
            by_rows(hidden),
            by_rows(width),
            whole(mixed.shape),
            whole(mlp.shape),
            whole(inner.shape),
            by_rows(128),
            whole(gm.shape),
            whole(wo.shape),
            whole(wu.shape),
            whole(wd.shape),
        ],
        out_specs=[
            by_rows(width),
            by_rows(width),
            pl.BlockSpec((8, chunk), lambda i: (0, jnp.minimum(i, chunks - 1))),
            pl.BlockSpec((width, width), lambda i: (jnp.clip(i - chunks, 0, 2 * slabs - 1), 0)),
            whole((width, width)),
            whole((8, width)),
        ],
        out_shape=[
            jax.ShapeDtypeStruct((rows, width), F32),
            jax.ShapeDtypeStruct((rows, width), BF16),
            jax.ShapeDtypeStruct((8, rows), F32),
            jax.ShapeDtypeStruct((2 * hidden, width), BF16),
            jax.ShapeDtypeStruct((width, width), BF16),
            jax.ShapeDtypeStruct((8, width), F32),
        ],
        scratch_shapes=[pltpu.VMEM((rows, hidden), BF16), pltpu.VMEM((rows, width), BF16)],
        compiler_params=params(),
        name="mlp_back",
    )(cot, slope, state, mixed, mlp, inner, inv, gm, wo, wu, wd)


def attention_back_kernel(tiles, scale, info_ref, q_ref, datt_ref, delta_ref, wk_ref, wv_ref, gain_ref, *refs):
    count = len(tiles)
    k_refs, v_refs, t_refs, w_refs = (refs[j * count : (j + 1) * count] for j in range(4))
    refs = refs[4 * count :]
    dtok_refs = refs[:count]
    dq_ref, dwk_ref, dwv_ref, dgain_ref, akey_ref, aval_ref = refs[count:]
    i = pl.program_id(0)
    width = q_ref.shape[1]

    @pl.when(i == 0)
    def _():
        dq_ref[...] = jnp.zeros_like(dq_ref)
        akey_ref[...] = jnp.zeros_like(akey_ref)
        aval_ref[...] = jnp.zeros_like(aval_ref)
        dgain_ref[...] = jnp.zeros_like(dgain_ref)

    first = 0
    for p in range(count):
        t = i - first
        inside = (t >= 0) & (t < tiles[p])
        active = inside & (t >= info_ref[3 + 3 * p]) & (t < info_ref[4 + 3 * p])

        @pl.when(active)
        def _(p=p):
            keys, weights = k_refs[p][...], w_refs[p][...]
            d_prob = dot(v_refs[p][...], datt_ref[...], NT)
            d_score = (weights.astype(F32) * (d_prob - delta_ref[:1, :])).astype(BF16)
            d_key = (dot(d_score, q_ref[...]) * scale).astype(BF16)
            d_value = dot(weights, datt_ref[...]).astype(BF16)
            dq_ref[...] += dot(d_score, keys, TN)
            unit, _ = norm_parts(t_refs[p][...].astype(F32))
            low = (unit * gain_ref[...]).astype(BF16)
            d_tok = dot(d_key, wk_ref[...], NT) + dot(d_value, wv_ref[...], NT)
            dtok_refs[p][...] = d_tok.astype(BF16)
            dgain_ref[...] += jnp.sum((d_tok * unit).reshape(TILE // 8, 8, width), axis=0)
            akey_ref[...] += dot(low, d_key, TN)
            aval_ref[...] += dot(low, d_value, TN)

        @pl.when(inside & jnp.logical_not(active))
        def _(p=p):
            dtok_refs[p][...] = jnp.zeros_like(dtok_refs[p])

        first += tiles[p]

    @pl.when(i == first - 1)
    def _():
        dwk_ref[...] = akey_ref[...].astype(BF16)
        dwv_ref[...] = aval_ref[...].astype(BF16)


def attention_back(info, q, datt, delta, wk, wv, gain, keys, values, tokens, weights, scale):
    rows, width = q.shape
    tiles = [k.shape[0] // TILE for k in keys]
    firsts = [sum(tiles[:p]) for p in range(len(tiles))]

    def tiled(p, columns):
        return pl.BlockSpec((TILE, columns), lambda i, *_: (jnp.clip(i - firsts[p], 0, tiles[p] - 1), 0))

    every = range(len(tiles))
    return pl.pallas_call(
        functools.partial(attention_back_kernel, tiles, scale),
        grid_spec=pltpu.PrefetchScalarGridSpec(
            num_scalar_prefetch=1,
            grid=(sum(tiles),),
            in_specs=[whole(a.shape) for a in (q, datt, delta, wk, wv, gain)]
            + [tiled(p, width) for _ in range(3) for p in every]
            + [tiled(p, rows) for p in every],
            out_specs=[tiled(p, width) for p in every]
            + [whole((rows, width)), whole((width, width)), whole((width, width)), whole((8, width))],
            scratch_shapes=[pltpu.VMEM((width, width), F32), pltpu.VMEM((width, width), F32)],
        ),
        out_shape=[jax.ShapeDtypeStruct(k.shape, BF16) for k in keys]
        + [
            jax.ShapeDtypeStruct((rows, width), F32),
            jax.ShapeDtypeStruct((width, width), BF16),
            jax.ShapeDtypeStruct((width, width), BF16),
            jax.ShapeDtypeStruct((8, width), F32),
        ],
        compiler_params=params(),
        name="attention_back",
    )(info, q, datt, delta, wk, wv, gain, *keys, *values, *tokens, *weights)


def latent_back_kernel(chunks, scale, dq_ref, lat_ref, dstate_ref, gain_ref, wq_ref, dlat_ref, dwq_ref, dgain_ref, acc_ref):
    i = pl.program_id(0)
    unit, inverse = norm_parts(lat_ref[...].astype(F32))
    gain = gain_ref[...]
    low = (unit * gain).astype(BF16)
    d_query = (dq_ref[...] * scale).astype(BF16)
    d_low = dot(d_query, wq_ref[...], NT)
    dlat_ref[...] = (dstate_ref[...] + norm_back(d_low, unit, inverse, gain)).astype(BF16)
    part = jnp.sum((d_low * unit).reshape(unit.shape[0] // 8, 8, unit.shape[1]), axis=0)
    dgain_ref[...] = jnp.where(i == 0, part, dgain_ref[...] + part)
    d_w = dot(low, d_query, TN)
    acc_ref[...] = jnp.where(i == 0, d_w, acc_ref[...] + d_w)

    @pl.when(i == chunks - 1)
    def _():
        dwq_ref[...] = acc_ref[...].astype(BF16)


def latent_back(dq, lat, dstate, gain, wq, scale):
    rows, width = lat.shape
    chunk = min(rows, TILE)
    block = pl.BlockSpec((chunk, width), lambda i: (i, 0))
    return pl.pallas_call(
        functools.partial(latent_back_kernel, rows // chunk, scale),
        grid=(rows // chunk,),
        in_specs=[block, block, block, whole(gain.shape), whole(wq.shape)],
        out_specs=[block, whole((width, width)), whole((8, width))],
        out_shape=[
            jax.ShapeDtypeStruct((rows, width), BF16),
            jax.ShapeDtypeStruct((width, width), BF16),
            jax.ShapeDtypeStruct((8, width), F32),
        ],
        scratch_shapes=[pltpu.VMEM((width, width), F32)],
        compiler_params=params(),
        name="latent_back",
    )(dq, lat, dstate, gain, wq)


def token_back_kernel(count, tok_ref, gain_ref, *refs):
    unit, inverse = norm_parts(tok_ref[...].astype(F32))
    total = refs[0][...].astype(F32)
    for ref in refs[1:count]:
        total = total + ref[...].astype(F32)
    refs[count][...] = norm_back(total, unit, inverse, gain_ref[...])


def token_back(tok, gain, parts):
    rows, width = tok.shape
    block = pl.BlockSpec((TILE, width), lambda i: (i, 0))
    return pl.pallas_call(
        functools.partial(token_back_kernel, len(parts)),
        grid=(rows // TILE,),
        in_specs=[block, whole(gain.shape)] + [block] * len(parts),
        out_specs=block,
        out_shape=jax.ShapeDtypeStruct((rows, width), F32),
        compiler_params=params(),
        name="token_back",
    )(tok, gain, *parts)


def exchange(value, blocks, flip):
    return lax.ppermute(value, "blk", [(i, i ^ flip) for i in range(blocks)])


def local(
    blocks, latents, tokens, lengths, gain_lat, gain_tok, gain_mlp, w_query, w_key, w_value, w_out, w_up, w_down, d_out
):
    lat, tok, cot = latents[0], tokens[0], d_out[0]
    scene_lengths = lengths[0]
    scenes = scene_lengths.shape[0]
    group = blocks // scenes
    span, width = tok.shape
    rows = lat.shape[0]
    part = rows // scenes
    scale = width ** (-0.5)
    position = lax.axis_index("blk")
    scene, member = position // group, position % group
    gl, gt, gm = (g.reshape(1, width) for g in (gain_lat, gain_tok, gain_mlp))

    order = jnp.arange(scenes, dtype=jnp.int32)
    begin = jnp.sum(jnp.where(order < scene, scene_lengths, 0))
    end = begin + jnp.sum(jnp.where(order == scene, scene_lengths, 0))

    def to_scenes(value):
        by_scene = jnp.swapaxes(value.reshape(part, scenes, width), 0, 1)
        moved = []
        for k in range(scenes):
            mine = lax.dynamic_index_in_dim(by_scene, scene ^ k, 0, keepdims=False)
            moved.append(exchange(mine, blocks, group * k) if k else mine)
        return jnp.concatenate(moved, axis=0)

    def from_scenes(value):
        moved = []
        for k in range(scenes):
            mine = value[k * part : (k + 1) * part]
            moved.append(exchange(mine, blocks, group * k) if k else mine)
        stacked = jnp.stack(moved, axis=0)
        stacked = jnp.stack([lax.dynamic_index_in_dim(stacked, scene ^ j, 0, keepdims=False) for j in range(scenes)], 1)
        return stacked.reshape(rows, width)

    lat_set = to_scenes(lat)
    pieces = [tok] + [exchange(tok, blocks, k) for k in range(1, group)]
    tail_rows = (scenes - 1) * group * span // 8
    tail_parts = []
    taken = 0
    while taken < tail_rows:
        owner = group - 1 - taken // span
        size = min(span, tail_rows - taken)
        block = pieces[0]
        for k in range(1, group):
            block = jnp.where(member == owner ^ k, pieces[k], block)
        tail_parts.insert(0, block[span - size :])
        taken += size
    tail = jnp.concatenate(tail_parts, axis=0) if len(tail_parts) > 1 else tail_parts[0]
    forward_pairs = [(i, i + group) for i in range(blocks - group)]
    tail = lax.ppermute(tail, "blk", forward_pairs)
    cot_set = to_scenes(cot)

    tok_set = [tail] + pieces[1:] + pieces[:1]
    starts = [scene * group * span - tail_rows]
    starts += [(scene * group + (member ^ k)) * span for k in [*range(1, group), 0]]
    entries = [begin, end]
    for piece, start in zip(tok_set, starts):
        tiles = piece.shape[0] // TILE
        entries += [
            start,
            jnp.clip((begin - start) // TILE, 0, tiles),
            jnp.clip((end - start + TILE - 1) // TILE, 0, tiles),
        ]
    info = jnp.stack(entries).astype(jnp.int32)

    keys, values = zip(*[keys_values(piece, gt, w_key, w_value) for piece in tok_set])
    query, mixed, mlp, state, inner, slope, out_set, inv, *weights = forward(
        info, lat_set, gl, gm, w_query, w_out, w_up, w_down, keys, values, scale
    )
    output = from_scenes(out_set)
    d_state, d_att, delta, mlp_pack, d_wo, dg_mlp = mlp_back(
        cot_set, slope, state, mixed, mlp, inner, inv, gm, w_out, w_up, w_down
    )
    *d_toks, dq, d_wk, d_wv, dg_tok = attention_back(
        info, query, d_att, delta, w_key, w_value, gt, keys, values, tok_set, weights, scale
    )
    d_lat_set, d_wq, dg_lat = latent_back(dq, lat_set, d_state, gl, w_query, scale)
    d_latents = from_scenes(d_lat_set).astype(F32)

    d_tail = lax.ppermute(d_toks[0], "blk", [(j, i) for i, j in forward_pairs])
    own_parts = [d_toks[-1]]
    returned = {k: d_toks[k] for k in range(1, group)}
    tail_own = []
    taken = 0
    while taken < tail_rows:
        owner = group - 1 - taken // span
        size = min(span, tail_rows - taken)
        chunk = d_tail[tail_rows - taken - size : tail_rows - taken]
        chunk = jnp.pad(chunk, ((span - size, 0), (0, 0)))
        tail_own.append((owner, chunk))
        taken += size
    for owner, chunk in tail_own:
        for k in range(1, group):
            returned[k] = returned[k] + jnp.where(member == owner ^ k, chunk, 0)
        own_parts.append(jnp.where(member == owner, chunk, 0))
    own_parts += [exchange(returned[k], blocks, k) for k in range(1, group)]
    d_tokens = token_back(tok, gt, own_parts)

    axes = ("seq", "blk")
    mlp_sum = lax.psum(mlp_pack, axes).astype(F32)
    small_sum = lax.psum(jnp.concatenate([d_wq, d_wk, d_wv, d_wo], axis=0), axes).astype(F32)
    gains = lax.psum(jnp.stack([jnp.sum(g, axis=0) for g in (dg_lat, dg_tok, dg_mlp)]), axes)
    hidden = w_up.shape[1]
    d_w_down = mlp_sum[:hidden]
    d_w_up = jnp.swapaxes(mlp_sum[hidden:].reshape(hidden // width, width, width), 0, 1).reshape(width, hidden)
    return (
        output[None],
        d_latents[None],
        d_tokens[None],
        small_sum[:width],
        small_sum[width : 2 * width],
        small_sum[2 * width : 3 * width],
        small_sum[3 * width :],
        d_w_up,
        d_w_down,
        gains[0],
        gains[1],
        gains[2],
    )


def solution(mesh):
    split = P("seq", "blk", None)
    in_specs = (split, split, P("seq", None)) + (P(),) * 9 + (split,)
    out_specs = (split,) * 3 + (P(),) * 9
    return jax.shard_map(
        functools.partial(local, mesh.shape["blk"]), mesh=mesh, in_specs=in_specs, out_specs=out_specs, check_vma=False
    )
```

time: 1310 us -> 425 us (0.32)
  waiting for transfers between devices: 575 us -> 131 us
  local copies, waits for them, and re-layouts: 266 us -> 26.5 us
  matrix products: 200 us -> 0 us
  Pallas kernels: 0 us -> 108 us
  blocking collectives: 172 us -> 68 us
  starting transfers between devices: 0.21 us -> 60 us
  other arithmetic: 40.9 us -> 12.8 us
  loops' own time: 27 us -> 0 us
    reduce_scatter x2 -> x0, waiting for transfers between devices: 236 us -> none  [the longest x1 127 us: local(): lax.psum_scatter(latent_order(d_query_sets).astype(jnp.bfloat16), 'blk',...]
    dot_general x46 -> x0, matrix products: 200 us -> none  [the longest x18 77.6 us: dot_rows(): lax.dot_general(left, right, (((1,), (1,)), ((), ())), preferred_element_...]
    all_gather x2 -> x0, waiting for transfers between devices: 167 us -> none  [the longest x1 121 us: local(): all_query = lax.all_gather(query, 'blk', axis=0, tiled=True)]
    pallas_call x0 -> x8, Pallas kernels: none -> 108 us  [the longest x1 36.5 us: forward(): pl.pallas_call(functools.partial(forward_kernel, pieces, scale), grid_spe...]
    psum x1, waiting for transfers between devices: 172 us -> 73.7 us  [local(): lax.psum(jnp.concatenate([d_wq, d_wk, d_wv, d_wo], axis=0), axes)]
    reshape x15 -> x1, local copies, waits for them, and re-layouts: 84.7 us -> 2.45 us  [local(): jnp.swapaxes(mlp_sum[hidden:].reshape(hidden // width, width, width), 0, 1)]
    dynamic_slice x20 -> x0, local copies, waits for them, and re-layouts: 75.8 us -> none  [the longest x12 71.2 us: scene_part(): return lax.dynamic_index_in_dim(grid, scene_id, 1, keepdims=False)]
    all_gather x2 -> x0, blocking collectives: 61.8 us -> none  [the longest x1 31 us: local(): lax.all_gather(delta, 'blk', axis=0, tiled=True)]
  transfers between devices with their start and end apart: 5 -> 17, of which waited for: 5 -> 5; matrix products, arithmetic and copies ran while one was open for 6% -> 6% of each run, Pallas kernels for 0% -> 3%
where the time goes in v1:
time: 425 us; the launch traced here: 424 us
  waiting for transfers between devices  131 us (31%)
  Pallas kernels  108 us (25%)
  blocking collectives  68 us (16%)
  starting transfers between devices  60 us (14%)
  local copies, waits for them, and re-layouts  26.5 us (6%)
  between operations  17.8 us (4%)
  other arithmetic  12.8 us (3%)
    psum x1, waiting for transfers between devices, local(): lax.psum(jnp.concatenate([d_wq, d_wk, d_wv, d_wo], axis=0), axes)  73.7 us
    psum x1, blocking collectives, local(): lax.psum(jnp.stack([jnp.sum(g, axis=0) for g in (dg_lat, dg_tok, dg_mlp)]...  68 us
    ppermute x14, starting transfers between devices, exchange(): return lax.ppermute(value, 'blk', [(i, i ^ flip) for i in range(blocks)])  53.9 us
    ppermute x14, waiting for transfers between devices, exchange(): return lax.ppermute(value, 'blk', [(i, i ^ flip) for i in range(blocks)])  44.1 us
    pallas_call x1, Pallas kernels, forward(): pl.pallas_call(functools.partial(forward_kernel, pieces, scale), grid_spe...  36.5 us
    pallas_call x1, Pallas kernels, mlp_back(): pl.pallas_call(functools.partial(mlp_back_kernel, chunks, slabs), grid=(c...  23.1 us
    pallas_call x1, Pallas kernels, attention_back(): pl.pallas_call(functools.partial(attention_back_kernel, tiles, scale), gr...  23 us
    pallas_call x3, Pallas kernels, keys_values(): pl.pallas_call(kv_kernel, grid=(rows // TILE,), in_specs=[block, whole(ga...  14.3 us
  transfers between devices with their start and end apart: 17, of which 5 were waited for; matrix products, arithmetic and copies ran while one was open for 6% of the time, Pallas kernels for 3%

profile of v1, /device:TPU:0, one launch (start us, length us, event | category | flops | bytes accessed | tf_op | source)
XLA Modules:
  0.0 424.0 jit_solution(499622581239765217)
XLA Ops:
  7.2 0.0 copy-start.1
  7.2 0.0 all-reduce.4.cloned.1.call-start
  7.2 3.0 collective-permute-start.3
  10.3 1.3 reshape_squeeze.7
  11.6 22.0 %collective-permute-done.3.tok_ref.refs_7_ = bf16[1024,512]{1,0:T(8,128)(2,1)S(1)} collective-permute-done((bf16[1024,512]{1,0:T(8,128)(2,1)}, bf16[1024,512]{1,0:T(8,128)(2,1)S(1)}, u32[]{:S(2)}, u32[]{:S(2)}) %collective-permute-start.3) | collective-permute-done | bytes 1048608 | tf_op jit(solution)/shard_map/ppermute | solution.py:445
  33.6 1.0 slice_select_fusion
  34.7 4.6 %collective-permute-start.4 = (bf16[768,512]{1,0:T(8,128)(2,1)}, bf16[768,512]{1,0:T(8,128)(2,1)}, u32[]{:S(2)}, u32[]{:S(2)}) collective-permute-start(bf16[768,512]{1,0:T(8,128)(2,1)} %slice_select_fusion), channel_id=1, source_target_pairs={{0,2},{1,3},{2,4},{3,5},{4,6},{5,7},{8,10},{9,11},{10,12},{11,13},... | collective-permute-start | bytes 2359304 | tf_op jit(solution)/shard_map/ppermute | solution.py:499
  39.3 3.0 constant_dynamic-slice_fusion.3
  42.2 0.7 copy.71
  43.0 0.5 collective-permute-start.10
  43.5 1.8 collective-permute-start.8
  45.4 2.2 collective-permute-start.9
  47.6 0.3 reshape_squeeze.6
  47.9 2.2 constant_dynamic-slice_fusion.7
  50.0 0.0 copy-start.17
  50.1 0.0 copy-start.3
  50.1 0.6 collective-permute-start.2
  50.8 11.6 %collective-permute-done.10 = bf16[256,512]{1,0:T(8,128)(2,1)} collective-permute-done((bf16[256,512]{1,0:T(8,128)(2,1)}, bf16[256,512]{1,0:T(8,128)(2,1)}, u32[]{:S(2)}, u32[]{:S(2)}) %collective-permute-start.10) | collective-permute-done | bytes 262176 | tf_op jit(solution)/shard_map/ppermute | solution.py:445
  62.3 17.9 %collective-permute-start = (bf16[256,512]{1,0:T(8,128)(2,1)S(1)}, bf16[256,512]{1,0:T(8,128)(2,1)S(1)}, u32[]{:S(2)}, u32[]{:S(2)}) collective-permute-start(bf16[256,512]{1,0:T(8,128)(2,1)S(1)} %bitcast.93), channel_id=1, source_target_pairs={{0,2},{1,3},{2,0},{3,1},{4,6},{5,7},{6,4},{7,5},{8,10},{9,11},{10,... | collective-permute-start | bytes 786440 | tf_op jit(solution)/shard_map/ppermute | solution.py:445
  80.3 2.4 collective-permute-start.1
  82.7 0.6 fusion.2
  86.8 5.0 %keys_values.5 = (bf16[1024,512]{1,0:T(8,128)(2,1)}, bf16[1024,512]{1,0:T(8,128)(2,1)}) custom-call(bf16[1024,512]{1,0:T(8,128)(2,1)} %bitcast.82, f32[1,512]{1,0:T(1,128)} %bitcast.98, bf16[512,512]{1,0:T(8,128)(2,1)} %wk_ref.7, bf16[512,512]{1,0:T(8,128)(2,1)} %wv_ref.7), custom_call_target="tpu_custom_call" | custom-call | tf_op jit(solution)/shard_map/keys_values/pallas_call | solution.py:63
  91.8 1.3 stack.119.info_ref
  93.1 2.2 pad_maximum_fusion.4.cot_ref
  95.3 1.0 pad_maximum_fusion.1.lat_ref
  96.4 5.0 %keys_values.4 = (bf16[1024,512]{1,0:T(8,128)(2,1)}, bf16[1024,512]{1,0:T(8,128)(2,1)}) custom-call(bf16[1024,512]{1,0:T(8,128)(2,1)} %copy-done.2, f32[1,512]{1,0:T(1,128)} %bitcast.99, bf16[512,512]{1,0:T(8,128)(2,1)} %wk_ref.7, bf16[512,512]{1,0:T(8,128)(2,1)} %wv_ref.7), custom_call_target="tpu_custom_call" | custom-call | tf_op jit(solution)/shard_map/keys_values/pallas_call | solution.py:63
  101.3 4.3 %keys_values.3 = (bf16[768,512]{1,0:T(8,128)(2,1)}, bf16[768,512]{1,0:T(8,128)(2,1)}) custom-call(bf16[768,512]{1,0:T(8,128)(2,1)} %collective-permute-done.4.tok_ref.refs_6_, f32[1,512]{1,0:T(1,128)} %bitcast.100, bf16[512,512]{1,0:T(8,128)(2,1)} %wk_ref.7, bf16[512,512]{1,0:T(8,128)(2,1)} %wv_ref.7), custom_call_target="tpu_custom_call" | custom-call | tf_op jit(solution)/shard_map/keys_values/pallas_call | solution.py:63
  105.7 36.5 %forward.1 = (bf16[1024,512]{1,0:T(8,128)(2,1)}, bf16[1024,512]{1,0:T(8,128)(2,1)}, bf16[1024,512]{1,0:T(8,128)(2,1)}, f32[1024,512]{1,0:T(8,128)}, bf16[1024,20...) custom-call(s32[11]{0:T(128)} %stack.119.info_ref, ...), custom_call_target="tpu_custom_call" | custom-call | tf_op jit(solution)/shard_map/forward/pallas_call | solution.py:151
  142.2 23.1 %mlp_back.1 = (f32[1024,512]{1,0:T(8,128)}, bf16[1024,512]{1,0:T(8,128)(2,1)}, f32[8,1024]{1,0:T(8,128)}, bf16[4096,512]{1,0:T(8,128)(2,1)}, bf16[512,512]{1,0:T(8,128)(2,1)}, /*index=5*/f32[8,512]{1,0:T(8,128)}) custom-call(bf16[1024,512]{1,0:T(8,128)(2,1)} %pad_maximum_fusion.4.cot_ref, bf16[1024,2048]{1,0:T(8,128)(2,1)} %get-tuple-element.53.slope_ref, ...), custom_call_target="tpu_custom_call" | custom-call | tf_op jit(solution)/shard_map/mlp_back/pallas_call | solution.py:263
  165.2 23.0 %attention_back.1 = (bf16[768,512]{1,0:T(8,128)(2,1)}, bf16[1024,512]{1,0:T(8,128)(2,1)}, bf16[1024,512]{1,0:T(8,128)(2,1)}, f32[1024,512]{1,0:T(8,128)}, bf16[5...) custom-call(s32[11]{0:T(128)} %stack.119.info_ref, bf16[1024,512]{1,0:T(8,128)(2,1)} %get-tuple-element.52.q_ref, ...), custom_call_target="tpu_custom_call" | custom-call | tf_op jit(solution)/shard_map/attention_back/pallas_call | solution.py:360
  188.2 0.0 copy-start.10
  188.3 6.4 %latent_back.1 = (bf16[1024,512]{1,0:T(8,128)(2,1)}, bf16[512,512]{1,0:T(8,128)(2,1)}, f32[8,512]{1,0:T(8,128)}) custom-call(f32[1024,512]{1,0:T(8,128)} %get-tuple-element.64.dq_ref, bf16[1024,512]{1,0:T(8,128)(2,1)} %pad_maximum_fusion.1.lat_ref, f32[1024,512]{1,0:T(8,128)} %get-tuple-element.65.dstate_ref, f32[1,512]{1,0:T(1,128)} %bitcast.109, ...), custom_call_target="tpu_custom_call" | custom-call | tf_op jit(solution)/shard_map/latent_back/pallas_call | solution.py:406
  194.7 2.5 pad_maximum_fusion
  197.2 0.0 all-reduce.4.cloned.1.call-update
  197.2 0.0 copy-start.16
  197.3 0.0 copy-start.7
  197.3 1.4 collective-permute-start.14
  198.7 0.9 slice_bitcast_fusion.1
  199.6 17.1 %collective-permute-start.7 = (bf16[256,512]{1,0:T(8,128)(2,1)}, bf16[256,512]{1,0:T(8,128)(2,1)}, u32[]{:S(2)}, u32[]{:S(2)}) collective-permute-start(bf16[256,512]{1,0:T(8,128)(2,1)} %get-tuple-element.105), channel_id=1, source_target_pairs={{0,6},{1,7},{2,4},{3,5},{4,2},{5,3},{6,0},{7,1},{8,14},{9,15},{10,... | collective-permute-start | bytes 786440 | tf_op jit(solution)/shard_map/ppermute | solution.py:445
  216.7 0.6 collective-permute-start.5
  217.3 1.0 slice_bitcast_fusion
  218.3 3.8 collective-permute-start.13
  222.1 13.1 %collective-permute-done.14 = bf16[768,512]{1,0:T(8,128)(2,1)} collective-permute-done((bf16[768,512]{1,0:T(8,128)(2,1)}, bf16[768,512]{1,0:T(8,128)(2,1)}, u32[]{:S(2)}, u32[]{:S(2)}) %collective-permute-start.14) | collective-permute-done | bytes 786464 | tf_op jit(solution)/shard_map/ppermute | solution.py:529
  235.2 2.5 fusion
  237.7 1.0 collective-permute-start.15
  238.7 68.0 %psum.23 = f32[3,512]{1,0:T(4,128)S(1)} all-reduce(f32[3,512]{1,0:T(4,128)S(1)} %pad_maximum_fusion.6), channel_id=1, replica_groups=mesh['seq'=4,'blk'=8] {'seq','blk'}, use_global_device_ids=true, to_apply=%region_7.8 | all-reduce | flops 1536 | bytes 12288 | tf_op jit(solution)/shard_map/psum | solution.py:551
  306.7 0.9 collective-permute-start.12
  307.7 2.1 collective-permute-start.11
  309.8 0.6 fusion.5
  310.4 1.2 pad_maximum_fusion.2
  311.7 10.5 %collective-permute-done.12 = bf16[256,512]{1,0:T(8,128)(2,1)S(1)} collective-permute-done((bf16[256,512]{1,0:T(8,128)(2,1)S(1)}, bf16[256,512]{1,0:T(8,128)(2,1)S(1)}, u32[]{:S(2)}, u32[]{:S(2)}) %collective-permute-start.12) | collective-permute-done | bytes 262176 | tf_op jit(solution)/shard_map/ppermute | solution.py:445
  322.2 0.1 pad_maximum_fusion.5
  322.3 1.0 dynamic-slice_bitcast_fusion.3
  323.3 0.2 maximum_convert_fusion
  323.5 1.4 copy.52
  324.8 1.7 reshape.81
  326.6 1.2 pad_maximum_fusion.3
  327.8 0.8 copy.47
  328.6 1.1 broadcast_in_dim_reshape.3
  329.7 4.8 %token_back.1 = f32[1024,512]{1,0:T(8,128)} custom-call(bf16[1024,512]{1,0:T(8,128)(2,1)} %bitcast.84, f32[1,512]{1,0:T(1,128)} %bitcast.102, bf16[1024,512]{1,0:T(8,128)(2,1)} %get-tuple-element.67.refs_0_, bf16[1024,512]{1,0:T(8,128)(2,1)} %get-tuple-element.113.refs_1_, bf16[1024,512]{1,0:T(8,128)(2,1)} %collective-permute-done.15.refs_2_), custom_call_target="tpu_custom_call" | custom-call | tf_op jit(solution)/shard_map/token_back/pallas_call | solution.py:433
  334.5 73.7 %all-reduce.4.cloned.1.call-done = (bf16[2048,512]{1,0:T(8,128)(2,1)}, bf16[4096,512]{1,0:T(8,128)(2,1)}) async-done(((bf16[2048,512]{1,0:T(8,128)(2,1)}, bf16[4096,512]{1,0:T(8,128)(2,1)}), (bf16[2048,512]{1,0:T(8,128)(2,1)}, bf16[4096,512]{1,0:T(8,128)(2,1)})) %all-reduce.4.cloned.1.call-update) | async-done | bytes 6291472 | tf_op jit(solution)/shard_map/psum | solution.py:550
  408.2 3.9 fusion.4
  412.1 2.6 fusion.3
  414.7 2.5 copy.62
  (54 shorter events, 0.4 us)
Async XLA Ops:
  7.2 26.5 %copy-start.1 = (bf16[1,1024,512]{2,1,0:T(8,128)(2,1)S(1)}, bf16[1,1024,512]{2,1,0:T(8,128)(2,1)}, u32[]{:S(2)}) copy-start(bf16[1,1024,512]{2,1,0:T(8,128)(2,1)} %param.14) | copy-start | bytes 3145732
  7.2 401.0 %all-reduce.4.cloned.1.call-start = ((), (), s32[]{:S(2)}) async-start(), calls=%async_computation | async-start | bytes 12582912 | tf_op jit(solution)/shard_map/psum | solution.py:550
  7.2 26.4 %collective-permute-start.3 = (bf16[1024,512]{1,0:T(8,128)(2,1)}, bf16[1024,512]{1,0:T(8,128)(2,1)S(1)}, u32[]{:S(2)}, u32[]{:S(2)}) collective-permute-start(bf16[1024,512]{1,0:T(8,128)(2,1)} %bitcast.81), channel_id=1, source_target_pairs={{0,1},{1,0},{2,3},{3,2},{4,5},{5,4},{6,7},{7,6},{8,9},{9,8},{10,11... | collective-permute-start | bytes 3145736 | tf_op jit(solution)/shard_map/ppermute | solution.py:445
  33.6 8.6 %copy-start.2 = (bf16[1024,512]{1,0:T(8,128)(2,1)}, bf16[1024,512]{1,0:T(8,128)(2,1)S(1)}, u32[]{:S(2)}) copy-start(bf16[1024,512]{1,0:T(8,128)(2,1)S(1)} %collective-permute-done.3.tok_ref.refs_7_) | copy-start | bytes 3145732
  34.7 66.7 %collective-permute-start.4 = (bf16[768,512]{1,0:T(8,128)(2,1)}, bf16[768,512]{1,0:T(8,128)(2,1)}, u32[]{:S(2)}, u32[]{:S(2)}) collective-permute-start(bf16[768,512]{1,0:T(8,128)(2,1)} %slice_select_fusion), channel_id=1, source_target_pairs={{0,2},{1,3},{2,4},{3,5},{4,6},{5,7},{8,10},{9,11},{10,12},{11,13},... | collective-permute-start | bytes 2359304 | tf_op jit(solution)/shard_map/ppermute | solution.py:499
  42.2 5.3 %copy-start.5 = (bf16[1,1024,512]{2,1,0:T(8,128)(2,1)S(1)}, bf16[1,1024,512]{2,1,0:T(8,128)(2,1)}, u32[]{:S(2)}) copy-start(bf16[1,1024,512]{2,1,0:T(8,128)(2,1)} %param.13) | copy-start | bytes 3145732
  43.0 19.4 %collective-permute-start.10 = (bf16[256,512]{1,0:T(8,128)(2,1)}, bf16[256,512]{1,0:T(8,128)(2,1)}, u32[]{:S(2)}, u32[]{:S(2)}) collective-permute-start(bf16[256,512]{1,0:T(8,128)(2,1)} %bitcast.72), channel_id=1, source_target_pairs={{0,6},{1,7},{2,4},{3,5},{4,2},{5,3},{6,0},{7,1},{8,14},{9,15},{10,... | collective-permute-start | bytes 786440 | tf_op jit(solution)/shard_map/ppermute | solution.py:445
  43.5 36.7 %collective-permute-start.8 = (bf16[256,512]{1,0:T(8,128)(2,1)S(1)}, bf16[256,512]{1,0:T(8,128)(2,1)}, u32[]{:S(2)}, u32[]{:S(2)}) collective-permute-start(bf16[256,512]{1,0:T(8,128)(2,1)S(1)} %bitcast.94), channel_id=1, source_target_pairs={{0,2},{1,3},{2,0},{3,1},{4,6},{5,7},{6,4},{7,5},{8,10},{9,11},{10,... | collective-permute-start | bytes 786440 | tf_op jit(solution)/shard_map/ppermute | solution.py:445
  45.4 47.7 %collective-permute-start.9 = (bf16[256,512]{1,0:T(8,128)(2,1)S(1)}, bf16[256,512]{1,0:T(8,128)(2,1)}, u32[]{:S(2)}, u32[]{:S(2)}) collective-permute-start(bf16[256,512]{1,0:T(8,128)(2,1)S(1)} %bitcast.90), channel_id=1, source_target_pairs={{0,4},{1,5},{2,6},{3,7},{4,0},{5,1},{6,2},{7,3},{8,12},{9,13},{10,... | collective-permute-start | bytes 786440 | tf_op jit(solution)/shard_map/ppermute | solution.py:445
  50.0 32.6 %copy-start.17 = (s32[1,4]{1,0:T(1,128)S(1)}, s32[1,4]{1,0:T(1,128)}, u32[]{:S(2)}) copy-start(s32[1,4]{1,0:T(1,128)} %param.15) | copy-start | bytes 52
  50.1 36.6 %copy-start.3 = (bf16[256,1,512]{2,1,0:T(2,128)(2,1)S(1)}, bf16[256,1,512]{2,1,0:T(2,128)(2,1)}, u32[]{:S(2)}) copy-start(bf16[256,1,512]{2,1,0:T(2,128)(2,1)} %get-tuple-element.96) | copy-start | bytes 786436
  50.1 45.2 %collective-permute-start.2 = (bf16[256,512]{1,0:T(8,128)(2,1)S(1)}, bf16[256,512]{1,0:T(8,128)(2,1)S(1)}, u32[]{:S(2)}, u32[]{:S(2)}) collective-permute-start(bf16[256,512]{1,0:T(8,128)(2,1)S(1)} %bitcast.92), channel_id=1, source_target_pairs={{0,6},{1,7},{2,4},{3,5},{4,2},{5,3},{6,0},{7,1},{8,14},{9,15},{10,... | collective-permute-start | bytes 786440 | tf_op jit(solution)/shard_map/ppermute | solution.py:445
  62.3 33.0 %collective-permute-start = (bf16[256,512]{1,0:T(8,128)(2,1)S(1)}, bf16[256,512]{1,0:T(8,128)(2,1)S(1)}, u32[]{:S(2)}, u32[]{:S(2)}) collective-permute-start(bf16[256,512]{1,0:T(8,128)(2,1)S(1)} %bitcast.93), channel_id=1, source_target_pairs={{0,2},{1,3},{2,0},{3,1},{4,6},{5,7},{6,4},{7,5},{8,10},{9,11},{10,... | collective-permute-start | bytes 786440 | tf_op jit(solution)/shard_map/ppermute | solution.py:445
  80.3 15.1 %collective-permute-start.1 = (bf16[256,512]{1,0:T(8,128)(2,1)S(1)}, bf16[256,512]{1,0:T(8,128)(2,1)S(1)}, u32[]{:S(2)}, u32[]{:S(2)}) collective-permute-start(bf16[256,512]{1,0:T(8,128)(2,1)S(1)} %bitcast.91), channel_id=1, source_target_pairs={{0,4},{1,5},{2,6},{3,7},{4,0},{5,1},{6,2},{7,3},{8,12},{9,13},{10,... | collective-permute-start | bytes 786440 | tf_op jit(solution)/shard_map/ppermute | solution.py:445
  188.2 6.5 %copy-start.9 = (bf16[512,512]{1,0:T(8,128)(2,1)S(1)}, bf16[512,512]{1,0:T(8,128)(2,1)}, u32[]{:S(2)}) copy-start(bf16[512,512]{1,0:T(8,128)(2,1)} %get-tuple-element.73) | copy-start | bytes 1572868
  188.2 6.4 %copy-start.10 = (bf16[512,512]{1,0:T(8,128)(2,1)S(1)}, bf16[512,512]{1,0:T(8,128)(2,1)}, u32[]{:S(2)}) copy-start(bf16[512,512]{1,0:T(8,128)(2,1)} %get-tuple-element.71) | copy-start | bytes 1572868
  188.2 6.4 %copy-start.11 = (bf16[512,512]{1,0:T(8,128)(2,1)S(1)}, bf16[512,512]{1,0:T(8,128)(2,1)}, u32[]{:S(2)}) copy-start(bf16[512,512]{1,0:T(8,128)(2,1)} %get-tuple-element.72) | copy-start | bytes 1572868
  197.2 1.5 copy-start.6
  197.2 20.0 %copy-start.16 = (f32[8,512]{1,0:T(8,128)S(1)}, f32[8,512]{1,0:T(8,128)}, u32[]{:S(2)}) copy-start(f32[8,512]{1,0:T(8,128)} %get-tuple-element.75) | copy-start | bytes 49156
  197.2 20.0 %copy-start.15 = (f32[8,512]{1,0:T(8,128)S(1)}, f32[8,512]{1,0:T(8,128)}, u32[]{:S(2)}) copy-start(f32[8,512]{1,0:T(8,128)} %get-tuple-element.76) | copy-start | bytes 49156
  197.3 20.1 %copy-start.14 = (f32[8,512]{1,0:T(8,128)S(1)}, f32[8,512]{1,0:T(8,128)}, u32[]{:S(2)}) copy-start(f32[8,512]{1,0:T(8,128)} %get-tuple-element.77) | copy-start | bytes 49156
  197.3 20.1 %copy-start.7 = (bf16[1024,512]{1,0:T(8,128)(2,1)S(1)}, bf16[1024,512]{1,0:T(8,128)(2,1)}, u32[]{:S(2)}) copy-start(bf16[1024,512]{1,0:T(8,128)(2,1)} %get-tuple-element.66) | copy-start | bytes 3145732
  197.3 37.9 %collective-permute-start.14 = (bf16[768,512]{1,0:T(8,128)(2,1)}, bf16[768,512]{1,0:T(8,128)(2,1)}, u32[]{:S(2)}, u32[]{:S(2)}) collective-permute-start(bf16[768,512]{1,0:T(8,128)(2,1)} %get-tuple-element.68), channel_id=1, source_target_pairs={{2,0},{3,1},{4,2},{5,3},{6,4},{7,5},{10,8},{11,9},{12,10},{13,11},... | collective-permute-start | bytes 2359304 | tf_op jit(solution)/shard_map/ppermute | solution.py:529
  198.7 36.5 %copy-start.4 = (bf16[1024,512]{1,0:T(8,128)(2,1)S(1)}, bf16[1024,512]{1,0:T(8,128)(2,1)}, u32[]{:S(2)}) copy-start(bf16[1024,512]{1,0:T(8,128)(2,1)} %get-tuple-element.69) | copy-start | bytes 3145732
  199.6 107.1 %collective-permute-start.7 = (bf16[256,512]{1,0:T(8,128)(2,1)}, bf16[256,512]{1,0:T(8,128)(2,1)}, u32[]{:S(2)}, u32[]{:S(2)}) collective-permute-start(bf16[256,512]{1,0:T(8,128)(2,1)} %get-tuple-element.105), channel_id=1, source_target_pairs={{0,6},{1,7},{2,4},{3,5},{4,2},{5,3},{6,0},{7,1},{8,14},{9,15},{10,... | collective-permute-start | bytes 786440 | tf_op jit(solution)/shard_map/ppermute | solution.py:445
  216.7 91.0 %collective-permute-start.6 = (bf16[256,512]{1,0:T(8,128)(2,1)}, bf16[256,512]{1,0:T(8,128)(2,1)}, u32[]{:S(2)}, u32[]{:S(2)}) collective-permute-start(bf16[256,512]{1,0:T(8,128)(2,1)} %get-tuple-element.106), channel_id=1, source_target_pairs={{0,4},{1,5},{2,6},{3,7},{4,0},{5,1},{6,2},{7,3},{8,12},{9,13},{10,... | collective-permute-start | bytes 786440 | tf_op jit(solution)/shard_map/ppermute | solution.py:445
  216.7 93.7 %collective-permute-start.5 = (bf16[256,512]{1,0:T(8,128)(2,1)}, bf16[256,512]{1,0:T(8,128)(2,1)}, u32[]{:S(2)}, u32[]{:S(2)}) collective-permute-start(bf16[256,512]{1,0:T(8,128)(2,1)} %get-tuple-element.107), channel_id=1, source_target_pairs={{0,2},{1,3},{2,0},{3,1},{4,6},{5,7},{6,4},{7,5},{8,10},{9,11},{10,... | collective-permute-start | bytes 786440 | tf_op jit(solution)/shard_map/ppermute | solution.py:445
  218.3 88.4 %copy-start.13 = (bf16[256,512]{1,0:T(8,128)(2,1)S(1)}, bf16[256,512]{1,0:T(8,128)(2,1)}, u32[]{:S(2)}) copy-start(bf16[256,512]{1,0:T(8,128)(2,1)} %get-tuple-element.94) | copy-start | bytes 786436
  218.3 89.4 %copy-start.12 = (bf16[256,512]{1,0:T(8,128)(2,1)S(1)}, bf16[256,512]{1,0:T(8,128)(2,1)}, u32[]{:S(2)}) copy-start(bf16[256,512]{1,0:T(8,128)(2,1)} %get-tuple-element.95) | copy-start | bytes 786436
  218.3 93.3 %collective-permute-start.13 = (bf16[256,512]{1,0:T(8,128)(2,1)}, bf16[256,512]{1,0:T(8,128)(2,1)S(1)}, u32[]{:S(2)}, u32[]{:S(2)}) collective-permute-start(bf16[256,512]{1,0:T(8,128)(2,1)} %get-tuple-element.93), channel_id=1, source_target_pairs={{0,6},{1,7},{2,4},{3,5},{4,2},{5,3},{6,0},{7,1},{8,14},{9,15},{10,... | collective-permute-start | bytes 786440 | tf_op jit(solution)/shard_map/ppermute | solution.py:445
  235.2 87.0 %copy-start.8 = (bf16[1,256,512]{2,1,0:T(8,128)(2,1)S(1)}, bf16[1,256,512]{2,1,0:T(8,128)(2,1)}, u32[]{:S(2)}) copy-start(bf16[1,256,512]{2,1,0:T(8,128)(2,1)} %get-tuple-element.92) | copy-start | bytes 786436
  237.7 92.0 %collective-permute-start.15 = (bf16[1024,512]{1,0:T(8,128)(2,1)S(1)}, bf16[1024,512]{1,0:T(8,128)(2,1)}, u32[]{:S(2)}, u32[]{:S(2)}) collective-permute-start(bf16[1024,512]{1,0:T(8,128)(2,1)S(1)} %get-tuple-element.112), channel_id=1, source_target_pairs={{0,1},{1,0},{2,3},{3,2},{4,5},{5,4},{6,7},{7,6},{8,9},{9,8},{10,11... | collective-permute-start | bytes 3145736 | tf_op jit(solution)/shard_map/ppermute | solution.py:445
  306.7 15.4 %collective-permute-start.12 = (bf16[256,512]{1,0:T(8,128)(2,1)S(1)}, bf16[256,512]{1,0:T(8,128)(2,1)S(1)}, u32[]{:S(2)}, u32[]{:S(2)}) collective-permute-start(bf16[256,512]{1,0:T(8,128)(2,1)S(1)} %copy-done.13), channel_id=1, source_target_pairs={{0,4},{1,5},{2,6},{3,7},{4,0},{5,1},{6,2},{7,3},{8,12},{9,13},{10,... | collective-permute-start | bytes 786440 | tf_op jit(solution)/shard_map/ppermute | solution.py:445
  307.7 14.5 %collective-permute-start.11 = (bf16[256,512]{1,0:T(8,128)(2,1)S(1)}, bf16[256,512]{1,0:T(8,128)(2,1)S(1)}, u32[]{:S(2)}, u32[]{:S(2)}) collective-permute-start(bf16[256,512]{1,0:T(8,128)(2,1)S(1)} %copy-done.12), channel_id=1, source_target_pairs={{0,2},{1,3},{2,0},{3,1},{4,6},{5,7},{6,4},{7,5},{8,10},{9,11},{10,... | collective-permute-start | bytes 786440 | tf_op jit(solution)/shard_map/ppermute | solution.py:445
  408.2 3.9 copy-start
Sparse Core Ops, SparseCore 0:
  197.3 210.8 all-reduce.3
